TPU v7x, 1024 devices: a whole 4x8x16 slice. The times are simulated.
1024 devices in a mesh: ctx: 32 (over y, z_hi), exp: 8 (over z_lo, core), dp: 4 (over x).
Axes of the slice: x: 4, y: 8, z: 16 (z_hi: 4, z_lo: 4; z = z_hi * 4 + z_lo), core: 2. Of those that a mesh axis runs over, the one named last changes fastest.
Arguments:
- queries: bfloat16 [4, 4096, 4096], P('dp', 'ctx', 'exp'), may hold values from -250 to 250
- key_values: bfloat16 [4, 4096, 1024], P('dp', 'ctx', 'exp'), may hold values from -5 to 5
- out_weight: bfloat16 [4096, 2880], P('exp'), may hold values from -0.09375 to 0.09375
- resid: bfloat16 [4, 4096, 2880], P('dp', ('ctx', 'exp')), may hold values from -45 to 45
- norm_gain: float32 [2880], replicated, may hold values from 0.5 to 1.5
- expert_ids: int32 [4, 4096, 2], P('dp', ('ctx', 'exp')), may hold values from 0 to 7, all different within a row; in each aligned block of 16 rows (0 to 15, 16 to 31, ..., all dimensions but the last counted through in order) at most 8 rows name the same one
- route_weights: float32 [4, 4096, 2], P('dp', ('ctx', 'exp')), may hold values from 0.1 to 1
- w_gate_up: bfloat16 [8, 2, 2880, 1536], P('exp', None, None, 'dp'), may hold values from -0.109375 to 0.109375
- w_down: bfloat16 [8, 1536, 2880], P('exp', 'dp'), may hold values from -0.15625 to 0.15625
Outputs:
- attended: bfloat16 [4, 4096, 2880], P('dp', ('ctx', 'exp'))
- expert_mix: bfloat16 [4, 4096, 2880], P('dp', ('ctx', 'exp'))
Inputs may be any that keep to these rules, and one draw needn't show every extreme that they name: `expert_ids`: A token's 2 experts differ. In each aligned block of 16 rows (the tokens of one device) no expert is named by more than 8 rows.
All inputs are finite; a program needn't handle non-finite values.
Results may differ from a plain program's by a relative error of at most 0.02.
Values may be sent and summed in bfloat16 or wider, within the bound.
A program may use at most 32 MiB of HBM per device.

v0:
```python
import math

import jax
import jax.numpy as jnp
from jax import lax
from jax.sharding import PartitionSpec as P

HD = 64


def expert_slice(rows, gate_up, down_proj):
    gate_value = jnp.dot(rows, gate_up[0], preferred_element_type=jnp.float32)
    up_value = jnp.dot(rows, gate_up[1], preferred_element_type=jnp.float32)
    activation = (gate_value * jax.nn.sigmoid(1.702 * gate_value) * (up_value + 1.0)).astype(
        jnp.bfloat16
    )
    return jnp.dot(activation, down_proj, preferred_element_type=jnp.float32).astype(jnp.bfloat16)


def widest_divisor(length, limit):
    chosen_width = 1
    for candidate in range(1, min(length, limit) + 1):
        if length % candidate == 0:
            chosen_width = candidate
    return chosen_width


def shards(
    queries, key_values, out_weight, resid, norm_gain, expert_ids, route_weights, w_gate_up, w_down
):
    block_len = queries.shape[1]
    head_count = queries.shape[2] // HD
    score_scale = 1.0 / math.sqrt(HD)
    query_heads = queries[0].reshape(block_len, head_count, HD).transpose(1, 0, 2)
    query_pos = lax.axis_index("ctx") * block_len + jnp.arange(block_len, dtype=jnp.int32)
    initial = (
        jnp.full((head_count, block_len), -1e30, jnp.float32),
        jnp.zeros((head_count, block_len), jnp.float32),
        jnp.zeros((head_count, block_len, HD), jnp.float32),
    )
    first_row = jnp.int32(0)
    piece_rows = lax.all_gather(key_values, "ctx", axis=1, tiled=True)[0]
    piece_len = piece_rows.shape[0]
    block_width = widest_divisor(piece_len, 512)

    def key_step(status, key_offset):
        running_max, running_sum, weighted = status
        key_block = lax.dynamic_slice_in_dim(piece_rows, key_offset, block_width, 0)
        key_part = key_block[:, :HD]
        value_part = key_block[:, HD:]
        scores = (
            jnp.einsum("hqd,kd->hqk", query_heads, key_part, preferred_element_type=jnp.float32)
            * score_scale
        )
        key_pos = first_row + key_offset + jnp.arange(block_width, dtype=jnp.int32)
        visible = (key_pos[None, :] <= query_pos[:, None])[None]
        new_max = jnp.maximum(running_max, jnp.max(jnp.where(visible, scores, -1e30), axis=-1))
        probs = jnp.where(visible, jnp.exp(scores - new_max[..., None]), 0.0)
        decay = jnp.exp(running_max - new_max)
        running_sum = running_sum * decay + jnp.sum(probs, axis=-1)
        weighted = weighted * decay[..., None] + jnp.einsum(
            "hqk,kd->hqd",
            probs.astype(jnp.bfloat16),
            value_part,
            preferred_element_type=jnp.float32,
        )
        return ((new_max, running_sum, weighted), None)

    key_offsets = jnp.arange(piece_len // block_width, dtype=jnp.int32) * block_width
    folded, _ = lax.scan(key_step, initial, key_offsets)
    running_max, running_sum, weighted = folded
    attention = (
        (weighted / running_sum[..., None])
        .astype(jnp.bfloat16)
        .transpose(1, 0, 2)
        .reshape(block_len, head_count * HD)
    )
    token_rows = resid.shape[1]
    width_model = resid.shape[2]
    projected = lax.psum_scatter(
        jnp.dot(attention, out_weight, preferred_element_type=jnp.float32).astype(jnp.bfloat16),
        "exp",
        scatter_dimension=0,
        tiled=True,
    ).astype(jnp.float32)
    hidden_state = resid[0].astype(jnp.float32) + projected
    normed = (
        hidden_state
        * lax.rsqrt(jnp.mean(hidden_state * hidden_state, axis=-1, keepdims=True) + 1e-05)
        * norm_gain
    ).astype(jnp.bfloat16)
    expert_count = lax.axis_size("exp")
    slice_count = lax.axis_size("dp")
    route_count = expert_ids.shape[2]
    capacity = 2 * token_rows * route_count // expert_count
    chosen_ids = expert_ids[0].reshape(-1)
    matches = (chosen_ids[:, None] == jnp.arange(expert_count, dtype=jnp.int32)[None, :]).astype(
        jnp.int32
    )
    slot_index = jnp.sum((jnp.cumsum(matches, axis=0) - matches) * matches, axis=1)
    target_slot = chosen_ids * capacity + slot_index
    placement = (
        target_slot[:, None] == jnp.arange(expert_count * capacity, dtype=jnp.int32)[None, :]
    ).reshape(token_rows, route_count, expert_count * capacity)
    selector = jnp.sum(placement.astype(jnp.float32), axis=1).astype(jnp.bfloat16)
    combiner = jnp.sum(jnp.where(placement, route_weights[0][:, :, None], 0.0), axis=1)
    outgoing = jnp.einsum("ts,td->sd", selector, normed, preferred_element_type=jnp.float32).astype(
        jnp.bfloat16
    )
    gate_up = w_gate_up[0]
    down_proj = w_down[0]
    fanned_out = jnp.broadcast_to(
        outgoing.reshape(expert_count, 1, capacity, width_model),
        (expert_count, slice_count, capacity, width_model),
    ).reshape(expert_count * slice_count, capacity, width_model)
    arrived = lax.all_to_all(fanned_out, ("exp", "dp"), split_axis=0, concat_axis=0, tiled=True)
    partial_rows = expert_slice(arrived.reshape(-1, width_model), gate_up, down_proj).reshape(
        arrived.shape
    )
    returned = lax.all_to_all(partial_rows, ("exp", "dp"), split_axis=0, concat_axis=0, tiled=True)
    expert_sums = jnp.sum(
        returned.reshape(expert_count, slice_count, capacity, width_model).astype(jnp.float32),
        axis=1,
    )
    mixture = jnp.dot(
        combiner,
        expert_sums.reshape(expert_count * capacity, width_model),
        preferred_element_type=jnp.float32,
        precision=lax.Precision.HIGHEST,
    )
    return (projected.astype(jnp.bfloat16)[None], mixture.astype(jnp.bfloat16)[None])


def solution(mesh):
    return jax.shard_map(
        shards,
        mesh=mesh,
        in_specs=(
            P("dp", "ctx", "exp"),
            P("dp", "ctx", "exp"),
            P("exp", None),
            P("dp", ("ctx", "exp"), None),
            P(),
            P("dp", ("ctx", "exp"), None),
            P("dp", ("ctx", "exp"), None),
            P("exp", None, None, "dp"),
            P("exp", "dp", None),
        ),
        out_specs=(P("dp", ("ctx", "exp"), None), P("dp", ("ctx", "exp"), None)),
        check_vma=False,
    )
```

profile of v0, /device:TPU:1, one launch (start us, length us, event | category | flops | bytes accessed | tf_op | source)
XLA Modules:
  0.0 354.6 jit_solution(191949817286316227)
XLA Ops:
  7.2 1.6 copy.27
  9.0 1.0 copy.28
  10.0 113.9 %all-gather.2.cloned.1.call-done = bf16[1,4096,128]{1,2,0:T(8,128)(2,1)} async-done(((bf16[1,128,128]{1,2,0:T(8,128)(2,1)}), bf16[1,4096,128]{1,2,0:T(8,128)(2,1)}) %all-gather.2.cloned.1.call-update) | async-done | bytes 1048592 | tf_op jit(solution)/shard_map/all_gather | solution.py:42
  123.9 83.1 %while.15 = (s32[]{:T(128)}, f32[8,128]{1,0:T(8,128)S(1)}, f32[8,128]{1,0:T(8,128)S(1)}, f32[8,128,64]{1,2,0:T(8,128)S(1)}, s32[8]{0:T(128)S(1)}, /*index=5*/bf1...) while((s32[]{:T(128)}, f32[8,128]{1,0:T(8,128)S(1)}, ...), condition=%wide.region_3.4_spmd.clone, body=%wide.region_0.3_spmd.clone.sunk | while | flops 140252800 | bytes 7410895 | solution.py:70
  123.9 0.6 dynamic_slice.10
  126.4 0.6 iota_add_fusion.5
  127.1 0.1 broadcast_compare_fusion.2
  127.2 2.8 fusion.74
  130.0 2.0 fusion.75
  132.0 2.2 convolution_add_fusion.2
  134.3 0.6 dynamic_slice.10
  136.8 0.6 iota_add_fusion.5
  137.5 0.1 broadcast_compare_fusion.2
  137.6 2.8 fusion.74
  140.4 2.0 fusion.75
  142.4 2.2 convolution_add_fusion.2
  144.7 0.6 dynamic_slice.10
  147.2 0.6 iota_add_fusion.5
  147.9 0.1 broadcast_compare_fusion.2
  148.0 2.8 fusion.74
  150.8 2.0 fusion.75
  152.8 2.2 convolution_add_fusion.2
  155.1 0.6 dynamic_slice.10
  157.6 0.6 iota_add_fusion.5
  158.3 0.1 broadcast_compare_fusion.2
  158.4 2.8 fusion.74
  161.2 2.0 fusion.75
  163.2 2.2 convolution_add_fusion.2
  165.5 0.6 dynamic_slice.10
  168.0 0.6 iota_add_fusion.5
  168.7 0.1 broadcast_compare_fusion.2
  168.8 2.8 fusion.74
  171.6 2.0 fusion.75
  173.7 2.2 convolution_add_fusion.2
  175.9 0.6 dynamic_slice.10
  178.4 0.6 iota_add_fusion.5
  179.1 0.1 broadcast_compare_fusion.2
  179.2 2.8 fusion.74
  182.0 2.0 fusion.75
  184.0 2.2 convolution_add_fusion.2
  186.3 0.6 dynamic_slice.10
  188.8 0.6 iota_add_fusion.5
  189.5 0.1 broadcast_compare_fusion.2
  189.6 2.8 fusion.74
  192.4 2.0 fusion.75
  194.5 2.2 convolution_add_fusion.2
  196.7 0.6 dynamic_slice.10
  199.2 0.6 iota_add_fusion.5
  200.0 2.7 fusion.74
  202.8 2.0 fusion.75
  204.8 2.2 convolution_add_fusion.2
  207.1 2.0 convolution_convert_fusion.1
  209.4 0.2 select_reduce_fusion.1
  209.9 38.0 %reduce-scatter.2.cloned.1.call-done = bf16[16,2880]{1,0:T(8,128)(2,1)} async-done(((bf16[128,2880]{1,0:T(8,128)(2,1)}), bf16[16,2880]{1,0:T(8,128)(2,1)}) %reduce-scatter.2.cloned.1.call-update) | async-done | bytes 92176 | tf_op jit(solution)/shard_map/reduce_scatter | solution.py:80
  247.9 1.0 multiply_reduce_fusion
  249.0 1.2 fusion.16
  250.3 43.9 %all_to_all.10 = bf16[32,8,2880]{2,1,0:T(8,128)(2,1)S(1)} all-to-all(bf16[32,8,2880]{2,1,0:T(8,128)(2,1)S(1)} %bitcast.102), channel_id=1, replica_groups=mesh['ctx'=32,'exp'=8,'dp'=4] {'exp','dp'}, dimensions={0} | all-to-all | bytes 2949120 | tf_op jit(solution)/shard_map/all_to_all | solution.py:116
  294.2 1.2 copy-done.1
  295.4 1.0 fusion.21
  296.3 5.7 %convolution_convert_fusion = bf16[256,2880]{0,1:T(8,128)(2,1)} fusion(bf16[1,384,2880]{1,2,0:T(8,128)(2,1)} %param.19, bf16[1,2,2880,384]{3,2,1,0:T(8,128)(2,1)} %param.18, bf16[32,8,2880]{2,1,0:T(8,128)(2,1)} %copy-done.1, f32[256,384]{1,0:T(8,128)S(1)} %fusion.21), kind=kOutput, calls=%fused_computation.26 | convolution fusion | flops 1133985792 | bytes 7798784 | tf_op jit(solution)/shard_map/dot_general | solution.py:17
  302.1 2.6 copy.31
  304.7 41.7 %all_to_all.11 = bf16[32,8,2880]{2,1,0:T(8,128)(2,1)S(1)} all-to-all(bf16[32,8,2880]{2,1,0:T(8,128)(2,1)} %bitcast.103), channel_id=1, replica_groups=mesh['ctx'=32,'exp'=8,'dp'=4] {'exp','dp'}, dimensions={0} | all-to-all | bytes 2949120 | tf_op jit(solution)/shard_map/all_to_all | solution.py:120
  346.4 0.2 convert_reduce_fusion
  346.6 1.1 fusion.17
  (65 shorter events, 1.2 us)
Async XLA Ops:
  7.2 199.9 %copy-start = (bf16[512,2880]{0,1:T(8,128)(2,1)S(1)}, bf16[512,2880]{0,1:T(8,128)(2,1)}, u32[]{:S(2)}) copy-start(bf16[512,2880]{0,1:T(8,128)(2,1)} %param.13) | copy-start | bytes 8847364
  7.2 116.7 %all-gather.2.cloned.1.call-start = ((), (), s32[]{:S(2)}) async-start(), calls=%async_computation.3 | async-start | bytes 1081344 | tf_op jit(solution)/shard_map/all_gather | solution.py:42
  8.9 239.0 %reduce-scatter.2.cloned.1.call-start = ((), (), s32[]{:S(2)}) async-start(), calls=%async_computation.4 | async-start | bytes 847872 | tf_op jit(solution)/shard_map/reduce_scatter | solution.py:80
  207.1 2.1 copy-start.4
  207.1 2.7 copy-start.5
  207.1 40.8 %copy-start.2 = (bf16[1,16,2880]{2,1,0:T(8,128)(2,1)S(1)}, bf16[1,16,2880]{2,1,0:T(8,128)(2,1)}, u32[]{:S(2)}) copy-start(bf16[1,16,2880]{2,1,0:T(8,128)(2,1)} %param.14) | copy-start | bytes 276484
  207.1 41.8 %copy-start.3 = (f32[2880]{0:T(1024)S(1)}, f32[2880]{0:T(1024)}, u32[]{:S(2)}) copy-start(f32[2880]{0:T(1024)} %param.15) | copy-start | bytes 34564
  250.2 45.2 %copy-start.6 = (bf16[1,2,2880,384]{3,2,1,0:T(8,128)(2,1)S(1)}, bf16[1,2,2880,384]{3,2,1,0:T(8,128)(2,1)}, u32[]{:S(2)}) copy-start(bf16[1,2,2880,384]{3,2,1,0:T(8,128)(2,1)} %param.18) | copy-start | bytes 13271044
  294.2 1.2 copy-start.1
Sparse Core Ops, SparseCore 0:
  12.8 111.0 all-gather.1
  209.3 38.6 reduce-scatter.1
where the time goes:
time: 356 us; the launch traced here: 355 us
  waiting for transfers between devices  152 us (43%)
  blocking collectives  85.7 us (24%)
  matrix products  50.8 us (14%)
  other arithmetic  24.3 us (7%)
  loops' own time  16 us (4%)
  between operations  14.2 us (4%)
  local copies, waits for them, and re-layouts  11.6 us (3%)
    all_gather x1, waiting for transfers between devices, shards(): piece_rows = lax.all_gather(key_values, 'ctx', axis=1, tiled=True)[0]  114 us
    all_to_all x1, blocking collectives, shards(): lax.all_to_all(fanned_out, ('exp', 'dp'), split_axis=0, concat_axis=0, ti...  43.9 us
    all_to_all x1, blocking collectives, shards(): lax.all_to_all(partial_rows, ('exp', 'dp'), split_axis=0, concat_axis=0,...  41.7 us
    reduce_scatter x1, waiting for transfers between devices, shards(): lax.psum_scatter(jnp.dot(attention, out_weight, preferred_element_type=jn...  38 us
    dot_general x8, matrix products, key_step(): jnp.einsum('hqd,kd->hqk', query_heads, key_part, preferred_element_type=j...  22.2 us
    dot_general x8, matrix products, key_step(): jnp.einsum('hqk,kd->hqd', probs.astype(jnp.bfloat16), value_part, preferr...  17.6 us
    reduce_sum x8, other arithmetic, key_step(): running_sum = running_sum * decay + jnp.sum(probs, axis=-1)  16.2 us
    another operation x1, loops' own time, shards(): folded, _ = lax.scan(key_step, initial, key_offsets)  16 us
  transfers between devices with their start and end apart: 2, of which 2 were waited for; matrix products, arithmetic and copies ran while one was open for 0% of the time, Pallas kernels for 0%

commit v1 on v0

v1 whole, which is shorter than its diff:
```python
import functools
import math

import jax
import jax.numpy as jnp
from jax import lax
from jax.experimental import pallas as pl
from jax.experimental.pallas import tpu as pltpu
from jax.sharding import PartitionSpec as P

HD = 64
YS = 8
ZH = 4
ZL = 4
XS = 4
MESH = pl.DeviceIdType.MESH
F32 = jnp.float32
BF16 = jnp.bfloat16
SCALE = math.log2(math.e) / math.sqrt(HD)
VMEM_BYTES = 56 * 1024 * 1024


def push(src, dst, send_sem, recv_sem, device):
    return pltpu.make_async_remote_copy(
        src_ref=src,
        dst_ref=dst,
        send_sem=send_sem,
        recv_sem=recv_sem,
        device_id=device,
        device_id_type=MESH,
    )


def column_tiles(width, step):
    return [(start, min(step, width - start)) for start in range(0, width, step)]


def barrier_with(devices):
    barrier = pltpu.get_barrier_semaphore()
    for device in devices:
        pl.semaphore_signal(barrier, inc=1, device_id=device, device_id_type=MESH)
    pl.semaphore_wait(barrier, len(devices))


def attention_kernel(
    q_ref,
    kv_ref,
    w_hbm,
    resid_ref,
    gain_ref,
    ids_ref,
    rw_ref,
    attended_ref,
    payload_ref,
    kv_all,
    qt,
    vt,
    top,
    acc,
    attn,
    w_ref,
    part,
    sib,
    mine,
    landed,
    w_sem,
    kv_sem,
    z_send,
    z_recv,
    f_send,
    f_recv,
    b_send,
    b_recv,
    s_send,
    s_recv,
    r_send,
    r_recv,
):
    ctx = lax.axis_index("ctx")
    y, z = lax.div(ctx, ZH), lax.rem(ctx, ZH)
    exp = lax.axis_index("exp")
    zl, core = lax.div(exp, 2), lax.rem(exp, 2)
    tokens, width = q_ref.shape
    heads = width // HD
    cols = tokens * heads
    model = w_ref.shape[1]
    rows = resid_ref.shape[0]

    up = {"ctx": lax.rem(y + 1, YS) * ZH + z}
    down = {"ctx": lax.rem(y + YS - 1, YS) * ZH + z}
    z_peer = [{"ctx": y * ZH + lax.rem(z + d, ZH)} for d in range(ZH)]
    sibling = {"exp": zl * 2 + 1 - core}
    l_peer = [{"exp": lax.rem(zl + d, ZL) * 2 + core} for d in range(ZL)]

    w_copy = pltpu.make_async_copy(w_hbm, w_ref, w_sem)
    w_copy.start()
    own_copy = pltpu.make_async_copy(kv_ref, kv_all.at[y, z], kv_sem)
    own_copy.start()
    barrier_with([up, down, sibling] + z_peer[1:] + l_peer[1:])

    shift = [0, 1, 3, 2]
    column = [lax.rem(z + ZH - s, ZH) for s in shift]

    def block(group, j):
        return kv_all.at[group, column[j]]

    def forward(group, step, j):
        src = kv_ref if j == 0 and step == 0 else block(group, j)
        return push(src, block(group, j), f_send.at[step, j], f_recv.at[step, j], up)

    def backward(group, step, j):
        src = kv_ref if j == 0 and step == 0 else block(group, j)
        return push(src, block(group, j), b_send.at[step, j], b_recv.at[step, j], down)

    def z_push(j):
        return push(
            kv_ref, kv_all.at[y, z], z_send.at[j - 1], z_recv.at[j - 1], z_peer[shift[j]]
        )

    sends_up = y < YS - 1
    sends_down = y <= 2

    @pl.when(sends_up)
    def _():
        forward(y, 0, 0).start()

    @pl.when(sends_down)
    def _():
        backward(y, 0, 0).start()

    for j in (1, 2, 3):
        z_push(j).start()

    for pair in range(heads // 2):
        turned = q_ref[:, pair * 128 : pair * 128 + 128].astype(F32).T.astype(BF16)
        qt[0:HD, 2 * pair * tokens : (2 * pair + 1) * tokens] = turned[0:HD]
        qt[0:HD, (2 * pair + 1) * tokens : (2 * pair + 2) * tokens] = turned[HD:]
    qt[HD:, :] = jnp.zeros((128 - HD, cols), BF16)
    vt[HD:, :] = jnp.ones((vt.shape[0] - HD, vt.shape[1]), BF16)
    top[...] = jnp.full(top.shape, -1e30, F32)
    acc[...] = jnp.zeros(acc.shape, F32)
    own_copy.wait()

    def attend(group, masked):
        for b in range(ZH):
            turned = kv_all[group, b].astype(F32).T
            vt[0:HD, b * tokens : (b + 1) * tokens] = turned[HD:].astype(BF16)

        def tile(t, carry):
            lanes = pl.ds(pl.multiple_of(t * 256, 256), 256)
            keys = kv_all[group].reshape(ZH * tokens, 2 * HD)
            scores = jnp.dot(keys, qt[:, lanes], preferred_element_type=F32)
            if masked:
                key_pos = lax.broadcasted_iota(jnp.int32, scores.shape, 0)
                query_pos = lax.broadcasted_iota(jnp.int32, scores.shape, 1) % tokens + z * tokens
                scores = jnp.where(key_pos <= query_pos, scores, -1e30)
            old = top[:, lanes]
            new = jnp.maximum(old, jnp.max(scores, axis=0, keepdims=True))
            probs = jnp.exp2((scores - new) * SCALE).astype(BF16)
            decay = jnp.exp2((old - new) * SCALE)
            top[:, lanes] = new
            acc[:, lanes] = acc[:, lanes] * decay + jnp.dot(
                vt[...], probs, preferred_element_type=F32
            )
            return carry

        lax.fori_loop(0, cols // 256, tile, 0)

    for j in (1, 2, 3):
        z_push(j).wait_recv()

        @pl.when(sends_up)
        def _():
            forward(y, 0, j).start()

        @pl.when(sends_down)
        def _():
            backward(y, 0, j).start()

    attend(y, True)

    for step in (1, 2, 3, 4):
        group = y - step

        @pl.when(group >= 0)
        def _():
            for j in range(ZH):
                forward(group, step - 1, j).wait_recv()
                if step < 4:

                    @pl.when(sends_up)
                    def _():
                        forward(group, step, j).start()

            attend(group, False)

        if step < 4:
            wrapped = lax.rem(y + step, YS)

            @pl.when(wrapped <= 2)
            def _():
                for j in range(ZH):
                    backward(wrapped, step - 1, j).wait_recv()
                    if step < 3:
                        backward(wrapped, step, j).start()

                @pl.when(wrapped < y)
                def _():
                    attend(wrapped, False)

    for pair in range(heads // 2):
        at = 2 * pair * tokens
        both = acc[:, at : at + 2 * tokens]
        ratio = both[0:HD] / both[HD : HD + 1]
        stacked = jnp.concatenate([ratio[:, :tokens], ratio[:, tokens:]], axis=0)
        attn[:, pair * 128 : pair * 128 + 128] = stacked.T.astype(BF16)
    w_copy.wait()

    tiles = column_tiles(model, 768)

    def to_sibling(n):
        start, size = tiles[n]
        return push(
            part.at[1 - core, :, :, pl.ds(start, size)],
            sib.at[:, :, pl.ds(start, size)],
            s_send.at[n],
            s_recv.at[n],
            sibling,
        )

    for n, (start, size) in enumerate(tiles):
        out = jnp.dot(attn[...], w_ref[:, start : start + size], preferred_element_type=F32)
        out = out.astype(BF16)
        for d in range(2 * ZL):
            part[d % 2, d // 2, :, start : start + size] = out[d * rows : (d + 1) * rows]
        to_sibling(n).start()
    for n, (start, size) in enumerate(tiles):
        to_sibling(n).wait_recv()
        both = part[core, :, :, start : start + size].astype(F32) + sib[
            :, :, start : start + size
        ].astype(F32)
        mine[:, :, start : start + size] = both.astype(BF16)

    def to_chip(d):
        return push(
            mine.at[lax.rem(zl + d, ZL)],
            landed.at[d - 1],
            r_send.at[d - 1],
            r_recv.at[d - 1],
            l_peer[d],
        )

    for d in (2, 1, 3):
        to_chip(d).start()
    for d in (1, 3, 2):
        to_chip(d).wait_recv()
    projected = mine[zl].astype(F32)
    for d in range(ZL - 1):
        projected = projected + landed[d].astype(F32)
    attended_ref[...] = projected.astype(BF16)
    hidden = resid_ref[...].astype(F32) + projected
    square = jnp.mean(hidden * hidden, axis=-1, keepdims=True)
    payload_ref[:, 0:model] = (hidden * lax.rsqrt(square + 1e-05) * gain_ref[...]).astype(BF16)
    spare = payload_ref.shape[1] - model
    place = lax.broadcasted_iota(jnp.int32, (rows, spare), 1)
    weight = jnp.zeros((rows, spare), F32)
    for k in range(ids_ref.shape[1]):
        weight = weight + jnp.where(ids_ref[:, k : k + 1] == place % 8, rw_ref[:, k : k + 1], 0.0)
    high = weight.astype(BF16).astype(F32)
    middle = (weight - high).astype(BF16).astype(F32)
    low = weight - high - middle
    terms = jnp.where(place < 8, high, jnp.where(place < 16, middle, low))
    payload_ref[:, model:] = jnp.where(place < 24, terms, 0.0).astype(BF16)

    for j in (1, 2, 3):
        z_push(j).wait_send()
    for j in range(ZH):

        @pl.when(sends_up)
        def _():
            forward(y, 0, j).wait_send()

        @pl.when(sends_down)
        def _():
            backward(y, 0, j).wait_send()

        for step in (1, 2, 3):

            @pl.when((y - step >= 0) & sends_up)
            def _():
                forward(y - step, step, j).wait_send()

        for step in (1, 2):

            @pl.when(lax.rem(y + step, YS) <= 2)
            def _():
                backward(lax.rem(y + step, YS), step, j).wait_send()

    for n in range(len(tiles)):
        to_sibling(n).wait_send()
    for d in (1, 2, 3):
        to_chip(d).wait_send()


def attention_part(q, kv, w, resid, gain, ids, rw):
    tokens, width = q.shape
    cols = tokens * width // HD
    model = w.shape[1]
    rows = resid.shape[0]
    padded = -(-model // 128) * 128
    tiles = len(column_tiles(model, 768))
    dma = pltpu.SemaphoreType.DMA
    vmem = pl.BlockSpec(memory_space=pltpu.VMEM)
    return pl.pallas_call(
        attention_kernel,
        out_shape=(
            jax.ShapeDtypeStruct((rows, model), BF16),
            jax.ShapeDtypeStruct((rows, padded), BF16),
        ),
        in_specs=[vmem, vmem, pl.BlockSpec(memory_space=pl.ANY), vmem, vmem, vmem, vmem],
        out_specs=(vmem, vmem),
        scratch_shapes=[
            pltpu.VMEM((YS, ZH, tokens, 2 * HD), BF16),
            pltpu.VMEM((2 * HD, cols), BF16),
            pltpu.VMEM((HD + 16, ZH * tokens), BF16),
            pltpu.VMEM((1, cols), F32),
            pltpu.VMEM((HD + 16, cols), F32),
            pltpu.VMEM((tokens, width), BF16),
            pltpu.VMEM((width, model), BF16),
            pltpu.VMEM((2, ZL, rows, model), BF16),
            pltpu.VMEM((ZL, rows, model), BF16),
            pltpu.VMEM((ZL, rows, model), BF16),
            pltpu.VMEM((ZL - 1, rows, model), BF16),
            dma,
            dma,
            dma((3,)),
            dma((3,)),
            dma((4, ZH)),
            dma((4, ZH)),
            dma((3, ZH)),
            dma((3, ZH)),
            dma((tiles,)),
            dma((tiles,)),
            dma((3,)),
            dma((3,)),
        ],
        compiler_params=pltpu.CompilerParams(
            collective_id=0, has_side_effects=True, vmem_limit_bytes=VMEM_BYTES
        ),
    )(q, kv, w, resid, gain, ids, rw)


def expert_kernel(
    payload_ref,
    wgu_hbm,
    wd_hbm,
    mix_ref,
    rows_all,
    wgu,
    wd,
    made,
    from_sib,
    from_left,
    from_right,
    relay_left,
    relay_right,
    total,
    ready,
    landed,
    w_sem,
    own_sem,
    z_send,
    z_recv,
    x_send,
    x_recv,
    o_send,
    o_recv,
    s_send,
    s_recv,
    p_send,
    p_recv,
    h_send,
    h_recv,
    r_send,
    r_recv,
):
    exp = lax.axis_index("exp")
    zl, core = lax.div(exp, 2), lax.rem(exp, 2)
    x = lax.axis_index("dp")
    rows, padded = payload_ref.shape
    model = mix_ref.shape[1]
    hidden = wd.shape[0]
    left, right = lax.rem(x + XS - 1, XS), lax.rem(x + 1, XS)
    far = lax.rem(x + 2, XS)
    to_left, to_right = {"dp": left}, {"dp": right}
    sibling = {"exp": zl * 2 + 1 - core}
    l_peer = [{"exp": lax.rem(zl + d, ZL) * 2 + core} for d in range(ZL)]

    own_copy = pltpu.make_async_copy(payload_ref, rows_all.at[x, zl, core], own_sem)
    own_copy.start()
    w_copies = [
        pltpu.make_async_copy(wgu_hbm.at[0], wgu.at[0:model, 0:hidden], w_sem.at[0]),
        pltpu.make_async_copy(wgu_hbm.at[1], wgu.at[0:model, hidden : 2 * hidden], w_sem.at[1]),
        pltpu.make_async_copy(wd_hbm, wd, w_sem.at[2]),
    ]
    for copy in w_copies:
        copy.start()
    barrier_with([to_left, to_right, sibling] + l_peer[1:])

    shift = [0, 1, 3, 2]
    column = [lax.rem(zl + ZL - s, ZL) for s in shift]

    def slot(xs, j, own=False):
        return rows_all.at[xs, column[j], core]

    def z_push(j):
        return push(
            payload_ref,
            rows_all.at[x, zl, core],
            z_send.at[j - 1],
            z_recv.at[j - 1],
            l_peer[shift[j]],
        )

    def source(j):
        return payload_ref if j == 0 else slot(x, j)

    def x_push(side, j):
        return push(
            source(j), slot(x, j), x_send.at[side, j], x_recv.at[side, j], (to_right, to_left)[side]
        )

    def x_arrived(side, j):
        at = slot((left, right)[side], j)
        push(at, at, x_send.at[side, j], x_recv.at[side, j], to_right).wait_recv()

    def o_push(j):
        at = slot(left if j < 2 else right, j)
        return push(at, at, o_send.at[j], o_recv.at[j], to_right if j < 2 else to_left)

    def o_arrived(j):
        at = slot(far, j)
        push(at, at, o_send.at[j], o_recv.at[j], to_right).wait_recv()

    columns = [x, left, right, far]

    def s_push(c, j):
        src = source(j) if c == 0 else slot(columns[c], j)
        return push(src, slot(columns[c], j), s_send.at[c, j], s_recv.at[c, j], sibling)

    def s_arrived(c, j):
        at = rows_all.at[columns[c], column[j], 1 - core]
        push(at, at, s_send.at[c, j], s_recv.at[c, j], sibling).wait_recv()

    x_push(0, 0).start()
    x_push(1, 0).start()
    for j in (1, 2, 3):
        z_push(j).start()
    s_push(0, 0).start()
    wgu[model:, :] = jnp.zeros((padded - model, 2 * hidden), BF16)

    for j in (1, 2, 3):
        z_push(j).wait_recv()
        x_push(0, j).start()
        x_push(1, j).start()
        s_push(0, j).start()
        for side in (0, 1):
            x_arrived(side, j - 1)
            if (j - 1 < 2) == (side == 0):
                o_push(j - 1).start()
            s_push(1 + side, j - 1).start()
    own_copy.wait()
    for copy in w_copies:
        copy.wait()

    tiles = column_tiles(model, 768)

    def expert(c):
        for j in range(ZL):
            s_arrived(c, j)
        at = columns[c]
        inputs = rows_all[at].reshape(2 * ZL * rows, padded)
        both = jnp.dot(inputs, wgu[...], preferred_element_type=F32)
        gate, up = both[:, :hidden], both[:, hidden:]
        tail = inputs[:, padded - 128 :].astype(F32)
        place = lax.broadcasted_iota(jnp.int32, tail.shape, 1) - (128 - (padded - model))
        chosen = (place == exp) | (place == exp + 8) | (place == exp + 16)
        weight = jnp.sum(jnp.where(chosen, tail, 0.0), axis=1, keepdims=True)
        active = (gate * jax.nn.sigmoid(1.702 * gate) * (up + 1.0) * weight).astype(BF16)
        for start, size in tiles:
            out = jnp.dot(active, wd[:, start : start + size], preferred_element_type=F32)
            out = out.astype(BF16)
            for d in range(2 * ZL):
                made[at, d % 2, d // 2, :, start : start + size] = out[d * rows : (d + 1) * rows]

    def p_push(c):
        return push(
            made.at[columns[c], 1 - core],
            from_sib.at[columns[c]],
            p_send.at[c],
            p_recv.at[c],
            sibling,
        )

    def pair_sum(c):
        p_push(c).wait_recv()
        at = columns[c]
        for b in range(ZL):
            made[at, core, b] = (made[at, core, b].astype(F32) + from_sib[at, b].astype(F32)).astype(
                BF16
            )

    def half(ref, h):
        return ref.at[2 * h : 2 * h + 2]

    def h_push(n):
        src, dst, device = [
            (half(made.at[right, core], 0), half(from_left, 0), to_right),
            (half(made.at[right, core], 1), half(from_left, 1), to_right),
            (half(made.at[left, core], 0), half(from_right, 0), to_left),
            (half(made.at[left, core], 1), half(from_right, 1), to_left),
            (half(made.at[far, core], 0), relay_left, to_right),
            (half(made.at[far, core], 1), relay_right, to_left),
        ][n]
        return push(src, dst, h_send.at[n], h_recv.at[n], device)

    expert(0)
    p_push(0).start()
    for side in (0, 1):
        x_arrived(side, 3)
        if side == 1:
            o_push(3).start()
        s_push(1 + side, 3).start()
    for j in range(ZL):
        o_arrived(j)
        s_push(3, j).start()
    expert(1)
    p_push(1).start()
    expert(2)
    p_push(2).start()
    pair_sum(1)
    h_push(2).start()
    expert(3)
    p_push(3).start()
    pair_sum(2)
    h_push(1).start()
    pair_sum(3)
    h_push(4).start()
    h_push(5).start()
    pair_sum(0)
    h_push(4).wait_recv()
    for b in (0, 1):
        made[right, core, b] = (made[right, core, b].astype(F32) + relay_left[b].astype(F32)).astype(
            BF16
        )
    h_push(0).start()
    h_push(5).wait_recv()
    for b in (0, 1):
        made[left, core, 2 + b] = (
            made[left, core, 2 + b].astype(F32) + relay_right[b].astype(F32)
        ).astype(BF16)
    h_push(3).start()

    h_push(1).wait_recv()
    h_push(2).wait_recv()
    h_push(0).wait_recv()
    h_push(3).wait_recv()
    for b in range(ZL):
        summed = (
            made[x, core, b].astype(F32) + from_left[b].astype(F32) + from_right[b].astype(F32)
        )
        total[b] = summed
        ready[b] = summed.astype(BF16)

    def to_chip(d):
        return push(
            ready.at[lax.rem(zl + d, ZL)],
            landed.at[d - 1],
            r_send.at[d - 1],
            r_recv.at[d - 1],
            l_peer[d],
        )

    for d in (2, 1, 3):
        to_chip(d).start()
    for d in (1, 3, 2):
        to_chip(d).wait_recv()
    summed = total[zl]
    for d in range(ZL - 1):
        summed = summed + landed[d].astype(F32)
    mix_ref[...] = summed.astype(BF16)

    for j in (1, 2, 3):
        z_push(j).wait_send()
    for j in range(ZL):
        for side in (0, 1):
            x_push(side, j).wait_send()
        o_push(j).wait_send()
        for c in range(4):
            s_push(c, j).wait_send()
    for c in range(4):
        p_push(c).wait_send()
    for n in range(6):
        h_push(n).wait_send()
    for d in (1, 2, 3):
        to_chip(d).wait_send()


def expert_part(payload, wgu, wd):
    rows, padded = payload.shape
    hidden, model = wd.shape
    dma = pltpu.SemaphoreType.DMA
    vmem = pl.BlockSpec(memory_space=pltpu.VMEM)
    anywhere = pl.BlockSpec(memory_space=pl.ANY)
    return pl.pallas_call(
        expert_kernel,
        out_shape=jax.ShapeDtypeStruct((rows, model), BF16),
        in_specs=[vmem, anywhere, anywhere],
        out_specs=vmem,
        scratch_shapes=[
            pltpu.VMEM((XS, ZL, 2, rows, padded), BF16),
            pltpu.VMEM((padded, 2 * hidden), BF16),
            pltpu.VMEM((hidden, model), BF16),
            pltpu.VMEM((XS, 2, ZL, rows, model), BF16),
            pltpu.VMEM((XS, ZL, rows, model), BF16),
            pltpu.VMEM((ZL, rows, model), BF16),
            pltpu.VMEM((ZL, rows, model), BF16),
            pltpu.VMEM((2, rows, model), BF16),
            pltpu.VMEM((2, rows, model), BF16),
            pltpu.VMEM((ZL, rows, model), F32),
            pltpu.VMEM((ZL, rows, model), BF16),
            pltpu.VMEM((ZL - 1, rows, model), BF16),
            dma((3,)),
            dma,
            dma((3,)),
            dma((3,)),
            dma((2, ZL)),
            dma((2, ZL)),
            dma((ZL,)),
            dma((ZL,)),
            dma((4, ZL)),
            dma((4, ZL)),
            dma((4,)),
            dma((4,)),
            dma((6,)),
            dma((6,)),
            dma((3,)),
            dma((3,)),
        ],
        compiler_params=pltpu.CompilerParams(
            collective_id=1, has_side_effects=True, vmem_limit_bytes=VMEM_BYTES
        ),
    )(payload, wgu, wd)


def shards(
    queries, key_values, out_weight, resid, norm_gain, expert_ids, route_weights, w_gate_up, w_down
):
    attended, payload = attention_part(
        queries[0],
        key_values[0],
        out_weight,
        resid[0],
        norm_gain[None],
        expert_ids[0],
        route_weights[0],
    )
    mixture = expert_part(payload, w_gate_up[0], w_down[0])
    return attended[None], mixture[None]


def solution(mesh):
    return jax.shard_map(
        shards,
        mesh=mesh,
        in_specs=(
            P("dp", "ctx", "exp"),
            P("dp", "ctx", "exp"),
            P("exp", None),
            P("dp", ("ctx", "exp"), None),
            P(),
            P("dp", ("ctx", "exp"), None),
            P("dp", ("ctx", "exp"), None),
            P("exp", None, None, "dp"),
            P("exp", "dp", None),
        ),
        out_specs=(P("dp", ("ctx", "exp"), None), P("dp", ("ctx", "exp"), None)),
        check_vma=False,
    )
```

time: 356 us -> 127 us (0.36)
  the two profiles are of different devices: /device:TPU:1 before, /device:TPU:58 now
where the time goes in v1:
time: 127 us
  Pallas kernels  115 us (91%)
  local copies, waits for them, and re-layouts  11.4 us (9%)
    pallas_call x1, Pallas kernels, attention_part(): pl.pallas_call(attention_kernel, out_shape=(jax.ShapeDtypeStruct((rows, m...  58.8 us
    pallas_call x1, Pallas kernels, expert_part(): pl.pallas_call(expert_kernel, out_shape=jax.ShapeDtypeStruct((rows, model...  56 us
    unnamed x14, local copies, waits for them, and re-layouts  9.39 us

profile of v1, /device:TPU:58, one launch (start us, length us, event | category | flops | bytes accessed | tf_op | source)
XLA Modules:
  0.0 126.8 jit_solution(11586105316652496686)
XLA Ops:
  0.6 0.0 copy-start.2
  0.6 0.0 copy-start.3
  0.7 0.0 copy-start.4
  0.7 4.6 %copy.11.w_hbm = bf16[512,2880]{1,0:T(8,128)(2,1)} copy(bf16[512,2880]{0,1:T(8,128)(2,1)} %param.11) | data formatting | bytes 5898240 | tf_op args[2]
  5.3 0.0 copy-done.2
  5.3 0.0 copy-start
  5.3 0.6 broadcast_in_dim.9.gain_ref
  5.9 0.0 copy-done.3
  5.9 0.7 copy.12.ids_ref
  6.6 0.0 copy-done.4
  6.6 0.7 copy.13.rw_ref
  7.2 58.8 %shard_map.104 = (bf16[16,2880]{1,0:T(8,128)(2,1)}, bf16[16,2944]{1,0:T(8,128)(2,1)}) custom-call(bf16[128,512]{1,0:T(8,128)(2,1)} %bitcast.12, bf16[128,128]{1,0:T(8,128)(2,1)} %bitcast.15, bf16[512,2880]{1,0:T(8,128)(2,1)} %copy.11.w_hbm, bf16[16,2880]{1,0:T(8,128)(2,1)} %bitcast.13, f32[1,2880]{1,0:T(1,128)} %broadcast_in_dim.9.gain_ref, ...), custom_call_target="tpu_custom_call" | custom-call | tf_op jit(solution)/shard_map/pallas_call | solution.py:314
  66.1 0.0 copy-done
  66.1 2.6 %copy.14 = bf16[1,384,2880]{2,1,0:T(8,128)(2,1)} copy(bf16[1,384,2880]{1,2,0:T(8,128)(2,1)S(1)} %copy-done) | data formatting | bytes 4423680 | tf_op args[8]
  68.7 0.0 copy-start.1
  68.7 56.0 %shard_map.105 = bf16[16,2880]{1,0:T(8,128)(2,1)} custom-call(bf16[16,2944]{1,0:T(8,128)(2,1)} %get-tuple-element.5.payload_ref, bf16[2,2880,384]{2,1,0:T(8,128)(2,1)} %bitcast.10, bf16[384,2880]{1,0:T(8,128)(2,1)} %bitcast.9), custom_call_target="tpu_custom_call" | custom-call | tf_op jit(solution)/shard_map/pallas_call | solution.py:615
  124.7 0.0 copy-done.1
  124.7 0.6 copy.17
  125.3 1.5 %copy.18 = bf16[1,16,2880]{2,1,0:T(8,128)(2,1)} copy(bf16[1,16,2880]{2,1,0:T(8,128)(2,1)} %bitcast.11) | data formatting | bytes 184320
Async XLA Ops:
  0.6 4.6 %copy-start.2 = (f32[2880]{0:T(1024)S(1)}, f32[2880]{0:T(1024)}, u32[]{:S(2)}) copy-start(f32[2880]{0:T(1024)} %param.13) | copy-start | bytes 34564
  0.6 5.2 %copy-start.3 = (s32[1,16,2]{1,2,0:T(2,128)S(1)}, s32[1,16,2]{1,2,0:T(2,128)}, u32[]{:S(2)}) copy-start(s32[1,16,2]{1,2,0:T(2,128)} %param.14) | copy-start | bytes 388
  0.7 5.9 %copy-start.4 = (f32[1,16,2]{1,2,0:T(2,128)S(1)}, f32[1,16,2]{1,2,0:T(2,128)}, u32[]{:S(2)}) copy-start(f32[1,16,2]{1,2,0:T(2,128)} %param.15) | copy-start | bytes 388
  5.3 60.8 %copy-start = (bf16[1,384,2880]{1,2,0:T(8,128)(2,1)S(1)}, bf16[1,384,2880]{1,2,0:T(8,128)(2,1)}, u32[]{:S(2)}) copy-start(bf16[1,384,2880]{1,2,0:T(8,128)(2,1)} %param.17) | copy-start | bytes 6635524
  68.7 56.0 %copy-start.1 = (bf16[16,2880]{1,0:T(8,128)(2,1)S(1)}, bf16[16,2880]{1,0:T(8,128)(2,1)}, u32[]{:S(2)}) copy-start(bf16[16,2880]{1,0:T(8,128)(2,1)} %get-tuple-element.4) | copy-start | bytes 276484

commit v2 on v0

v2 whole, which is shorter than its diff:
```python
import functools
import math

import jax
import jax.numpy as jnp
from jax import lax
from jax.experimental import pallas as pl
from jax.experimental.pallas import tpu as pltpu
from jax.sharding import PartitionSpec as P

HD = 64
YS = 8
ZH = 4
ZL = 4
XS = 4
MESH = pl.DeviceIdType.MESH
F32 = jnp.float32
BF16 = jnp.bfloat16
SCALE = math.log2(math.e) / math.sqrt(HD)
VMEM_BYTES = 56 * 1024 * 1024


def push(src, dst, send_sem, recv_sem, device):
    return pltpu.make_async_remote_copy(
        src_ref=src,
        dst_ref=dst,
        send_sem=send_sem,
        recv_sem=recv_sem,
        device_id=device,
        device_id_type=MESH,
    )


def column_tiles(width, step):
    return [(start, min(step, width - start)) for start in range(0, width, step)]


def barrier_with(devices):
    barrier = pltpu.get_barrier_semaphore()
    for device in devices:
        pl.semaphore_signal(barrier, inc=1, device_id=device, device_id_type=MESH)
    pl.semaphore_wait(barrier, len(devices))


def dot_t(a, b):
    return lax.dot_general(a, b, (((1,), (1,)), ((), ())), preferred_element_type=F32)


def layer_kernel(
    q_ref,
    kv_ref,
    wo_hbm,
    resid_ref,
    gain_ref,
    ids_ref,
    rw_ref,
    wgu_hbm,
    wd_hbm,
    attended_ref,
    mix_ref,
    kv_all,
    qt,
    vt,
    top,
    acc,
    attn,
    wo,
    part,
    sib,
    mine,
    landed,
    payload,
    rows_all,
    wgu,
    wd,
    made,
    from_sib,
    from_left,
    from_right,
    relay_left,
    relay_right,
    total,
    ready,
    returned,
    w_sem,
    own_sem,
    a_send,
    a_recv,
    f_send,
    f_recv,
    b_send,
    b_recv,
    e_send,
    e_recv,
    c_send,
    c_recv,
    z_send,
    z_recv,
    x_send,
    x_recv,
    o_send,
    o_recv,
    s_send,
    s_recv,
    p_send,
    p_recv,
    h_send,
    h_recv,
    r_send,
    r_recv,
):
    ctx = lax.axis_index("ctx")
    y, z = lax.div(ctx, ZH), lax.rem(ctx, ZH)
    exp = lax.axis_index("exp")
    zl, core = lax.div(exp, 2), lax.rem(exp, 2)
    x = lax.axis_index("dp")
    tokens, width = q_ref.shape
    heads = width // HD
    cols = tokens * heads
    rows, model = resid_ref.shape
    padded = payload.shape[1]
    hidden = wd.shape[1]
    tiles = column_tiles(model, 768)

    up = {"ctx": lax.rem(y + 1, YS) * ZH + z}
    down = {"ctx": lax.rem(y + YS - 1, YS) * ZH + z}
    z_peer = [{"ctx": y * ZH + lax.rem(z + d, ZH)} for d in range(ZH)]
    sibling = {"exp": zl * 2 + 1 - core}
    l_peer = [{"exp": lax.rem(zl + d, ZL) * 2 + core} for d in range(ZL)]
    left, right = lax.rem(x + XS - 1, XS), lax.rem(x + 1, XS)
    far = lax.rem(x + 2, XS)
    to_left, to_right = {"dp": left}, {"dp": right}

    w_copies = [
        pltpu.make_async_copy(wo_hbm, wo, w_sem.at[0]),
        pltpu.make_async_copy(wgu_hbm.at[0], wgu.at[0:model, 0:hidden], w_sem.at[1]),
        pltpu.make_async_copy(wgu_hbm.at[1], wgu.at[0:model, hidden : 2 * hidden], w_sem.at[2]),
        pltpu.make_async_copy(wd_hbm, wd, w_sem.at[3]),
    ]
    own_copy = pltpu.make_async_copy(kv_ref, kv_all.at[y, z], own_sem)
    own_copy.start()
    for copy in w_copies:
        copy.start()
    barrier_with([up, down, sibling, to_left, to_right] + z_peer[1:] + l_peer[1:])

    shift = [0, 1, 3, 2]
    started = []

    def gather_and_attend():
        column = [lax.rem(z + ZH - s, ZH) for s in shift]
        sends_up = y < YS - 1
        sends_down = y <= 2

        def block(group, j):
            return kv_all.at[group, column[j]]

        def forward(group, step, j):
            src = kv_ref if j == 0 and step == 0 else block(group, j)
            return push(src, block(group, j), f_send.at[step, j], f_recv.at[step, j], up)

        def backward(group, step, j):
            src = kv_ref if j == 0 and step == 0 else block(group, j)
            return push(src, block(group, j), b_send.at[step, j], b_recv.at[step, j], down)

        def z_push(j):
            return push(
                kv_ref, kv_all.at[y, z], a_send.at[j - 1], a_recv.at[j - 1], z_peer[shift[j]]
            )

        @pl.when(sends_up)
        def _():
            forward(y, 0, 0).start()

        @pl.when(sends_down)
        def _():
            backward(y, 0, 0).start()

        for j in (1, 2, 3):
            z_push(j).start()

        for pair in range(heads // 2):
            turned = q_ref[:, pair * 128 : pair * 128 + 128].astype(F32).T.astype(BF16)
            qt[0:HD, 2 * pair * tokens : (2 * pair + 1) * tokens] = turned[0:HD]
            qt[0:HD, (2 * pair + 1) * tokens : (2 * pair + 2) * tokens] = turned[HD:]
        qt[HD:, :] = jnp.zeros((128 - HD, cols), BF16)
        vt[HD:, :] = jnp.ones((vt.shape[0] - HD, vt.shape[1]), BF16)
        top[...] = jnp.full(top.shape, -1e30, F32)
        acc[...] = jnp.zeros(acc.shape, F32)
        wgu[model:, :] = jnp.zeros((padded - model, 2 * hidden), BF16)
        own_copy.wait()

        def attend(group, masked):
            for b in range(ZH):
                turned = kv_all[group, b].astype(F32).T
                vt[0:HD, b * tokens : (b + 1) * tokens] = turned[HD:].astype(BF16)
            keys = kv_all[group].reshape(ZH * tokens, 2 * HD)
            halves = [slice(0, cols // 2), slice(cols // 2, cols)]
            scores = [jnp.dot(keys, qt[:, lanes], preferred_element_type=F32) for lanes in halves]
            for lanes, seen in zip(halves, scores):
                if masked:
                    key_pos = lax.broadcasted_iota(jnp.int32, seen.shape, 0)
                    query_pos = lax.broadcasted_iota(jnp.int32, seen.shape, 1) % tokens + z * tokens
                    seen = jnp.where(key_pos <= query_pos, seen, -1e30)
                old = top[:, lanes]
                new = jnp.maximum(old, jnp.max(seen, axis=0, keepdims=True))
                probs = jnp.exp2((seen - new) * SCALE).astype(BF16)
                decay = jnp.exp2((old - new) * SCALE)
                top[:, lanes] = new
                acc[:, lanes] = acc[:, lanes] * decay + jnp.dot(
                    vt[...], probs, preferred_element_type=F32
                )

        for j in (1, 2, 3):
            z_push(j).wait_recv()

            @pl.when(sends_up)
            def _():
                forward(y, 0, j).start()

            @pl.when(sends_down)
            def _():
                backward(y, 0, j).start()

        attend(y, True)

        for step in (1, 2, 3, 4):
            group = y - step

            @pl.when(group >= 0)
            def _():
                for j in range(ZH):
                    forward(group, step - 1, j).wait_recv()
                    if step < 4:

                        @pl.when(sends_up)
                        def _():
                            forward(group, step, j).start()

                attend(group, False)

            if step < 4:
                wrapped = lax.rem(y + step, YS)

                @pl.when(wrapped <= 2)
                def _():
                    for j in range(ZH):
                        backward(wrapped, step - 1, j).wait_recv()
                        if step < 3:
                            backward(wrapped, step, j).start()

                    @pl.when(wrapped < y)
                    def _():
                        attend(wrapped, False)

        def finish():
            for j in (1, 2, 3):
                z_push(j).wait_send()
            for j in range(ZH):

                @pl.when(sends_up)
                def _():
                    forward(y, 0, j).wait_send()

                @pl.when(sends_down)
                def _():
                    backward(y, 0, j).wait_send()

                for step in (1, 2, 3):

                    @pl.when((y - step >= 0) & sends_up)
                    def _():
                        forward(y - step, step, j).wait_send()

                for step in (1, 2):

                    @pl.when(lax.rem(y + step, YS) <= 2)
                    def _():
                        backward(lax.rem(y + step, YS), step, j).wait_send()

        started.append(finish)

    def project():
        for pair in range(heads // 2):
            at = 2 * pair * tokens
            both = acc[:, at : at + 2 * tokens]
            ratio = both[0:HD] / both[HD : HD + 1]
            stacked = jnp.concatenate([ratio[:, :tokens], ratio[:, tokens:]], axis=0)
            attn[:, pair * 128 : pair * 128 + 128] = stacked.T.astype(BF16)
        w_copies[0].wait()

        def to_sibling(n):
            start, size = tiles[n]
            return push(
                part.at[1 - core, :, :, pl.ds(start, size)],
                sib.at[:, :, pl.ds(start, size)],
                e_send.at[n],
                e_recv.at[n],
                sibling,
            )

        for n, (start, size) in enumerate(tiles):
            out = dot_t(attn[...], wo[start : start + size, :]).astype(BF16)
            for d in range(2 * ZL):
                part[d % 2, d // 2, :, start : start + size] = out[d * rows : (d + 1) * rows]
            to_sibling(n).start()
        for n, (start, size) in enumerate(tiles):
            to_sibling(n).wait_recv()
            both = part[core, :, :, start : start + size].astype(F32) + sib[
                :, :, start : start + size
            ].astype(F32)
            mine[:, :, start : start + size] = both.astype(BF16)
        started.append(lambda: [to_sibling(n).wait_send() for n in range(len(tiles))])

    def sum_heads():
        def to_chip(d):
            return push(
                mine.at[lax.rem(zl + d, ZL)],
                landed.at[d - 1],
                c_send.at[d - 1],
                c_recv.at[d - 1],
                l_peer[d],
            )

        for d in (2, 1, 3):
            to_chip(d).start()
        for d in (1, 3, 2):
            to_chip(d).wait_recv()
        started.append(lambda: [to_chip(d).wait_send() for d in (1, 2, 3)])

    def norm():
        projected = mine[zl].astype(F32)
        for d in range(ZL - 1):
            projected = projected + landed[d].astype(F32)
        attended_ref[...] = projected.astype(BF16)
        state = resid_ref[...].astype(F32) + projected
        square = jnp.mean(state * state, axis=-1, keepdims=True)
        gain = gain_ref[...].reshape(1, model)
        payload[:, 0:model] = (state * lax.rsqrt(square + 1e-05) * gain).astype(BF16)
        spare = padded - model
        place = lax.broadcasted_iota(jnp.int32, (rows, spare), 1)
        same = lax.broadcasted_iota(jnp.int32, (rows, rows), 0) == lax.broadcasted_iota(
            jnp.int32, (rows, rows), 1
        )
        weight = jnp.zeros((rows, spare), F32)
        for k in range(ids_ref.shape[0]):
            named = jnp.sum(
                jnp.where(same, ids_ref[k : k + 1, :].astype(F32), 0.0), axis=1, keepdims=True
            )
            share = jnp.sum(jnp.where(same, rw_ref[k : k + 1, :], 0.0), axis=1, keepdims=True)
            weight = weight + jnp.where(named == (place % 8).astype(F32), share, 0.0)
        high = weight.astype(BF16).astype(F32)
        middle = (weight - high).astype(BF16).astype(F32)
        low = weight - high - middle
        terms = jnp.where(place < 8, high, jnp.where(place < 16, middle, low))
        payload[:, model:] = jnp.where(place < 24, terms, 0.0).astype(BF16)

    column = [lax.rem(zl + ZL - s, ZL) for s in shift]
    columns = [x, left, right, far]

    def slot(at, j):
        return rows_all.at[at, column[j], core]

    def expert(c):
        at = columns[c]
        inputs = rows_all[at].reshape(2 * ZL * rows, padded)
        both = jnp.dot(inputs, wgu[...], preferred_element_type=F32)
        gate, upper = both[:, :hidden], both[:, hidden:]
        tail = inputs[:, padded - 128 :].astype(F32)
        place = lax.broadcasted_iota(jnp.int32, tail.shape, 1) - (128 - (padded - model))
        chosen = (place == exp) | (place == exp + 8) | (place == exp + 16)
        weight = jnp.sum(jnp.where(chosen, tail, 0.0), axis=1, keepdims=True)
        active = (gate * jax.nn.sigmoid(1.702 * gate) * (upper + 1.0) * weight).astype(BF16)
        for start, size in tiles:
            out = dot_t(active, wd[start : start + size, :]).astype(BF16)
            for d in range(2 * ZL):
                made[at, d % 2, d // 2, :, start : start + size] = out[d * rows : (d + 1) * rows]

    def p_push(c):
        return push(
            made.at[columns[c], 1 - core],
            from_sib.at[columns[c]],
            p_send.at[c],
            p_recv.at[c],
            sibling,
        )

    def gather_and_apply():
        def z_push(j):
            return push(
                payload,
                rows_all.at[x, zl, core],
                z_send.at[j - 1],
                z_recv.at[j - 1],
                l_peer[shift[j]],
            )

        def source(j):
            return payload if j == 0 else slot(x, j)

        def x_push(side, j):
            device = (to_right, to_left)[side]
            return push(source(j), slot(x, j), x_send.at[side, j], x_recv.at[side, j], device)

        def x_arrived(side, j):
            at = slot((left, right)[side], j)
            push(at, at, x_send.at[side, j], x_recv.at[side, j], to_right).wait_recv()

        def o_push(j):
            at = slot(left if j < 2 else right, j)
            return push(at, at, o_send.at[j], o_recv.at[j], to_right if j < 2 else to_left)

        def o_arrived(j):
            at = slot(far, j)
            push(at, at, o_send.at[j], o_recv.at[j], to_right).wait_recv()

        def s_push(c, j):
            src = source(j) if c == 0 else slot(columns[c], j)
            return push(src, slot(columns[c], j), s_send.at[c, j], s_recv.at[c, j], sibling)

        def s_arrived(c, j):
            at = rows_all.at[columns[c], column[j], 1 - core]
            push(at, at, s_send.at[c, j], s_recv.at[c, j], sibling).wait_recv()

        own = pltpu.make_async_copy(payload, rows_all.at[x, zl, core], own_sem)
        own.start()
        x_push(0, 0).start()
        x_push(1, 0).start()
        for j in (1, 2, 3):
            z_push(j).start()
        s_push(0, 0).start()
        for j in (1, 2, 3):
            z_push(j).wait_recv()
            x_push(0, j).start()
            x_push(1, j).start()
            s_push(0, j).start()
            for side in (0, 1):
                x_arrived(side, j - 1)
                if (j - 1 < 2) == (side == 0):
                    o_push(j - 1).start()
                s_push(1 + side, j - 1).start()
        own.wait()
        for copy in w_copies[1:]:
            copy.wait()
        for j in range(ZL):
            s_arrived(0, j)
        expert(0)
        p_push(0).start()
        for side in (0, 1):
            x_arrived(side, 3)
            if side == 1:
                o_push(3).start()
            s_push(1 + side, 3).start()
        for j in range(ZL):
            o_arrived(j)
            s_push(3, j).start()
        for c in (1, 2, 3):
            for j in range(ZL):
                s_arrived(c, j)
            expert(c)
            p_push(c).start()

        def finish():
            for j in (1, 2, 3):
                z_push(j).wait_send()
            for j in range(ZL):
                for side in (0, 1):
                    x_push(side, j).wait_send()
                o_push(j).wait_send()
                for c in range(4):
                    s_push(c, j).wait_send()
            for c in range(4):
                p_push(c).wait_send()

        started.append(finish)

    def sum_columns():
        def pair_sum(c):
            p_push(c).wait_recv()
            at = columns[c]
            for b in range(ZL):
                made[at, core, b] = (
                    made[at, core, b].astype(F32) + from_sib[at, b].astype(F32)
                ).astype(BF16)

        def half(ref, h):
            return ref.at[2 * h : 2 * h + 2]

        def h_push(n):
            src, dst, device = [
                (half(made.at[right, core], 0), half(from_left, 0), to_right),
                (half(made.at[right, core], 1), half(from_left, 1), to_right),
                (half(made.at[left, core], 0), half(from_right, 0), to_left),
                (half(made.at[left, core], 1), half(from_right, 1), to_left),
                (half(made.at[far, core], 0), relay_left, to_right),
                (half(made.at[far, core], 1), relay_right, to_left),
            ][n]
            return push(src, dst, h_send.at[n], h_recv.at[n], device)

        pair_sum(1)
        h_push(2).start()
        pair_sum(2)
        h_push(1).start()
        pair_sum(3)
        h_push(4).start()
        h_push(5).start()
        pair_sum(0)
        h_push(4).wait_recv()
        for b in (0, 1):
            made[right, core, b] = (
                made[right, core, b].astype(F32) + relay_left[b].astype(F32)
            ).astype(BF16)
        h_push(0).start()
        h_push(5).wait_recv()
        for b in (0, 1):
            made[left, core, 2 + b] = (
                made[left, core, 2 + b].astype(F32) + relay_right[b].astype(F32)
            ).astype(BF16)
        h_push(3).start()
        for n in (1, 2, 0, 3):
            h_push(n).wait_recv()
        started.append(lambda: [h_push(n).wait_send() for n in range(6)])

    def sum_slices():
        for b in range(ZL):
            summed = (
                made[x, core, b].astype(F32) + from_left[b].astype(F32) + from_right[b].astype(F32)
            )
            total[b] = summed
            ready[b] = summed.astype(BF16)

        def to_chip(d):
            return push(
                ready.at[lax.rem(zl + d, ZL)],
                returned.at[d - 1],
                r_send.at[d - 1],
                r_recv.at[d - 1],
                l_peer[d],
            )

        for d in (2, 1, 3):
            to_chip(d).start()
        for d in (1, 3, 2):
            to_chip(d).wait_recv()
        summed = total[zl]
        for d in range(ZL - 1):
            summed = summed + returned[d].astype(F32)
        mix_ref[...] = summed.astype(BF16)
        started.append(lambda: [to_chip(d).wait_send() for d in (1, 2, 3)])

    gather_and_attend()
    project()
    sum_heads()
    norm()
    gather_and_apply()
    sum_columns()
    sum_slices()
    for finish in started:
        finish()


def layer(q, kv, wo, resid, gain, ids, rw, wgu, wd):
    tokens, width = q.shape
    cols = tokens * width // HD
    rows, model = resid.shape
    hidden = wd.shape[1]
    padded = -(-model // 128) * 128
    tiles = len(column_tiles(model, 768))
    dma = pltpu.SemaphoreType.DMA
    vmem = pl.BlockSpec(memory_space=pltpu.VMEM)
    hbm = pl.BlockSpec(memory_space=pl.ANY)
    return pl.pallas_call(
        layer_kernel,
        out_shape=(
            jax.ShapeDtypeStruct((rows, model), BF16),
            jax.ShapeDtypeStruct((rows, model), BF16),
        ),
        in_specs=[vmem, vmem, hbm, vmem, vmem, vmem, vmem, hbm, hbm],
        out_specs=(vmem, vmem),
        scratch_shapes=[
            pltpu.VMEM((YS, ZH, tokens, 2 * HD), BF16),
            pltpu.VMEM((2 * HD, cols), BF16),
            pltpu.VMEM((HD + 16, ZH * tokens), BF16),
            pltpu.VMEM((1, cols), F32),
            pltpu.VMEM((HD + 16, cols), F32),
            pltpu.VMEM((tokens, width), BF16),
            pltpu.VMEM((model, width), BF16),
            pltpu.VMEM((2, ZL, rows, model), BF16),
            pltpu.VMEM((ZL, rows, model), BF16),
            pltpu.VMEM((ZL, rows, model), BF16),
            pltpu.VMEM((ZL - 1, rows, model), BF16),
            pltpu.VMEM((rows, padded), BF16),
            pltpu.VMEM((XS, ZL, 2, rows, padded), BF16),
            pltpu.VMEM((padded, 2 * hidden), BF16),
            pltpu.VMEM((model, hidden), BF16),
            pltpu.VMEM((XS, 2, ZL, rows, model), BF16),
            pltpu.VMEM((XS, ZL, rows, model), BF16),
            pltpu.VMEM((ZL, rows, model), BF16),
            pltpu.VMEM((ZL, rows, model), BF16),
            pltpu.VMEM((2, rows, model), BF16),
            pltpu.VMEM((2, rows, model), BF16),
            pltpu.VMEM((ZL, rows, model), F32),
            pltpu.VMEM((ZL, rows, model), BF16),
            pltpu.VMEM((ZL - 1, rows, model), BF16),
            dma((4,)),
            dma,
        ]
        + [dma((3,))] * 2
        + [dma((4, ZH))] * 2
        + [dma((3, ZH))] * 2
        + [dma((tiles,))] * 2
        + [dma((3,))] * 2
        + [dma((3,))] * 2
        + [dma((2, ZL))] * 2
        + [dma((ZL,))] * 2
        + [dma((4, ZL))] * 2
        + [dma((4,))] * 2
        + [dma((6,))] * 2
        + [dma((3,))] * 2,
        compiler_params=pltpu.CompilerParams(
            collective_id=0, has_side_effects=True, vmem_limit_bytes=VMEM_BYTES
        ),
    )(q, kv, wo, resid, gain, ids, rw, wgu, wd)


def shards(
    queries, key_values, out_weight, resid, norm_gain, expert_ids, route_weights, w_gate_up, w_down
):
    attended, mixture = layer(
        queries[0],
        key_values[0],
        out_weight.T,
        resid[0],
        norm_gain,
        expert_ids[0].T,
        route_weights[0].T,
        w_gate_up[0],
        w_down[0].T,
    )
    return attended[None], mixture[None]


def solution(mesh):
    return jax.shard_map(
        shards,
        mesh=mesh,
        in_specs=(
            P("dp", "ctx", "exp"),
            P("dp", "ctx", "exp"),
            P("exp", None),
            P("dp", ("ctx", "exp"), None),
            P(),
            P("dp", ("ctx", "exp"), None),
            P("dp", ("ctx", "exp"), None),
            P("exp", None, None, "dp"),
            P("exp", "dp", None),
        ),
        out_specs=(P("dp", ("ctx", "exp"), None), P("dp", ("ctx", "exp"), None)),
        check_vma=False,
    )
```

time: 356 us -> 112 us (0.31)
  the two profiles are of different devices: /device:TPU:1 before, /device:TPU:58 now
where the time goes in v2:
time: 112 us
  Pallas kernels  108 us (96%)
  local copies, waits for them, and re-layouts  3.07 us (3%)
    pallas_call x1, Pallas kernels, layer(): pl.pallas_call(layer_kernel, out_shape=(jax.ShapeDtypeStruct((rows, model...  108 us
    unnamed x2, local copies, waits for them, and re-layouts  3.07 us

profile of v2, /device:TPU:58, one launch (start us, length us, event | category | flops | bytes accessed | tf_op | source)
XLA Modules:
  0.0 111.9 jit_solution(1366867141420052620)
XLA Ops:
  0.6 108.2 %shard_map.104 = (bf16[16,2880]{1,0:T(8,128)(2,1)}, bf16[16,2880]{1,0:T(8,128)(2,1)}) custom-call(bf16[128,512]{1,0:T(8,128)(2,1)} %bitcast.19, bf16[128,128]{1,0:T(8,128)(2,1)} %bitcast.23, bf16[2880,512]{1,0:T(8,128)(2,1)} %bitcast.17, bf16[16,2880]{1,0:T(8,128)(2,1)} %bitcast.20, f32[2880]{0:T(1024)} %gain_ref.1, s32[2,16]{1,0:T(2,128)} %bitcast.24, ...), custom_call_target="tpu_custom_call" | custom-call | tf_op jit(solution)/shard_map/pallas_call | solution.py:571
  108.9 1.5 %copy.13 = bf16[1,16,2880]{2,1,0:T(8,128)(2,1)} copy(bf16[1,16,2880]{2,1,0:T(8,128)(2,1)} %bitcast.22) | data formatting | bytes 184320
  110.4 1.5 %copy.14 = bf16[1,16,2880]{2,1,0:T(8,128)(2,1)} copy(bf16[1,16,2880]{2,1,0:T(8,128)(2,1)} %bitcast.21) | data formatting | bytes 184320

commit v3 on v2

--- a/solution.py
+++ b/solution.py
@@ -33,6 +33,12 @@
 
 def column_tiles(width, step):
     return [(start, min(step, width - start)) for start in range(0, width, step)]
+
+
+def column_pieces(model, padded):
+    cut = padded // 256 * 128
+    tiles = column_tiles(cut, 768) + [(cut + a, b) for a, b in column_tiles(model - cut, 768)]
+    return [(0, cut), (cut, padded - cut)], tiles
 
 
 def barrier_with(devices):
@@ -77,8 +83,7 @@
     from_sib,
     from_left,
     from_right,
-    relay_left,
-    relay_right,
+    relays,
     total,
     ready,
     returned,
@@ -102,8 +107,14 @@
     o_recv,
     s_send,
     s_recv,
+    t_send,
+    t_recv,
     p_send,
     p_recv,
+    g_send,
+    g_recv,
+    k_send,
+    k_recv,
     h_send,
     h_recv,
     r_send,
@@ -120,7 +131,7 @@
     rows, model = resid_ref.shape
     padded = payload.shape[1]
     hidden = wd.shape[1]
-    tiles = column_tiles(model, 768)
+    pieces, tiles = column_pieces(model, padded)
 
     up = {"ctx": lax.rem(y + 1, YS) * ZH + z}
     down = {"ctx": lax.rem(y + YS - 1, YS) * ZH + z}
@@ -309,33 +320,44 @@
                 :, :, start : start + size
             ].astype(F32)
             mine[:, :, start : start + size] = both.astype(BF16)
+            for piece in (0, 1):
+                if start + size == min(sum(pieces[piece]), model):
+                    for j in (1, 2, 3):
+                        to_chip(j, piece).start()
         started.append(lambda: [to_sibling(n).wait_send() for n in range(len(tiles))])
-
-    def sum_heads():
-        def to_chip(d):
-            return push(
-                mine.at[lax.rem(zl + d, ZL)],
-                landed.at[d - 1],
-                c_send.at[d - 1],
-                c_recv.at[d - 1],
-                l_peer[d],
-            )
-
-        for d in (2, 1, 3):
-            to_chip(d).start()
-        for d in (1, 3, 2):
-            to_chip(d).wait_recv()
-        started.append(lambda: [to_chip(d).wait_send() for d in (1, 2, 3)])
-
-    def norm():
-        projected = mine[zl].astype(F32)
-        for d in range(ZL - 1):
-            projected = projected + landed[d].astype(F32)
-        attended_ref[...] = projected.astype(BF16)
-        state = resid_ref[...].astype(F32) + projected
-        square = jnp.mean(state * state, axis=-1, keepdims=True)
-        gain = gain_ref[...].reshape(1, model)
-        payload[:, 0:model] = (state * lax.rsqrt(square + 1e-05) * gain).astype(BF16)
+        started.append(
+            lambda: [to_chip(j, piece).wait_send() for j in (1, 2, 3) for piece in (0, 1)]
+        )
+
+    def model_columns(piece):
+        start, size = pieces[piece]
+        return start, min(size, model - start)
+
+    def to_chip(j, piece):
+        lanes = pl.ds(*model_columns(piece))
+        return push(
+            mine.at[column[j], :, lanes],
+            landed.at[zl, :, lanes],
+            c_send.at[piece, j - 1],
+            c_recv.at[piece, zl],
+            {"exp": column[j] * 2 + core},
+        )
+
+    def finish_rows(piece, square):
+        start, size = model_columns(piece)
+        lanes = slice(start, start + size)
+        projected = mine[zl, :, lanes].astype(F32)
+        for j in (1, 2, 3):
+            at = landed.at[column[j], :, pl.ds(start, size)]
+            push(at, at, c_send.at[piece, 0], c_recv.at[piece, column[j]], sibling).wait_recv()
+            projected = projected + landed[column[j], :, lanes].astype(F32)
+        attended_ref[:, lanes] = projected.astype(BF16)
+        state = resid_ref[:, lanes].astype(F32) + projected
+        gain = gain_ref[lanes].reshape(1, size)
+        payload[:, lanes] = (state * gain).astype(BF16)
+        return square + jnp.sum(state * state, axis=-1, keepdims=True)
+
+    def finish_tail(square):
         spare = padded - model
         place = lax.broadcasted_iota(jnp.int32, (rows, spare), 1)
         same = lax.broadcasted_iota(jnp.int32, (rows, rows), 0) == lax.broadcasted_iota(
@@ -347,33 +369,44 @@
                 jnp.where(same, ids_ref[k : k + 1, :].astype(F32), 0.0), axis=1, keepdims=True
             )
             share = jnp.sum(jnp.where(same, rw_ref[k : k + 1, :], 0.0), axis=1, keepdims=True)
-            weight = weight + jnp.where(named == (place % 8).astype(F32), share, 0.0)
+            weight = weight + jnp.where(named == (place % 9).astype(F32), share, 0.0)
+        inverse = lax.rsqrt(square / model + 1e-05)
+        weight = jnp.where(place % 9 == 8, inverse, weight)
         high = weight.astype(BF16).astype(F32)
         middle = (weight - high).astype(BF16).astype(F32)
         low = weight - high - middle
-        terms = jnp.where(place < 8, high, jnp.where(place < 16, middle, low))
-        payload[:, model:] = jnp.where(place < 24, terms, 0.0).astype(BF16)
-
-    column = [lax.rem(zl + ZL - s, ZL) for s in shift]
+        terms = jnp.where(place < 9, high, jnp.where(place < 18, middle, low))
+        payload[:, model:] = jnp.where(place < 27, terms, 0.0).astype(BF16)
+
+    side = lax.div(zl, 2)
+    place_in = zl + side * (ZL - 1 - 2 * zl)
+    column = [zl]
+    for j in range(1, ZL):
+        at = j - 1 + lax.div(j - 1 + ZL - place_in, ZL)
+        column.append(at + side * (ZL - 1 - 2 * at))
     columns = [x, left, right, far]
 
-    def slot(at, j):
-        return rows_all.at[at, column[j], core]
+    def slot(at, j, piece):
+        return rows_all.at[at, core, column[j], :, pl.ds(*pieces[piece])]
 
     def expert(c):
         at = columns[c]
         inputs = rows_all[at].reshape(2 * ZL * rows, padded)
         both = jnp.dot(inputs, wgu[...], preferred_element_type=F32)
-        gate, upper = both[:, :hidden], both[:, hidden:]
         tail = inputs[:, padded - 128 :].astype(F32)
         place = lax.broadcasted_iota(jnp.int32, tail.shape, 1) - (128 - (padded - model))
-        chosen = (place == exp) | (place == exp + 8) | (place == exp + 16)
-        weight = jnp.sum(jnp.where(chosen, tail, 0.0), axis=1, keepdims=True)
+
+        def terms_of(n):
+            chosen = (place == n) | (place == n + 9) | (place == n + 18)
+            return jnp.sum(jnp.where(chosen, tail, 0.0), axis=1, keepdims=True)
+
+        weight, inverse = terms_of(exp), terms_of(8)
+        gate, upper = both[:, :hidden] * inverse, both[:, hidden:] * inverse
         active = (gate * jax.nn.sigmoid(1.702 * gate) * (upper + 1.0) * weight).astype(BF16)
-        for start, size in tiles:
+        for start, size in column_tiles(model, 768):
             out = dot_t(active, wd[start : start + size, :]).astype(BF16)
             for d in range(2 * ZL):
-                made[at, d % 2, d // 2, :, start : start + size] = out[d * rows : (d + 1) * rows]
+                made[at, d // ZL, d % ZL, :, start : start + size] = out[d * rows : (d + 1) * rows]
 
     def p_push(c):
         return push(
@@ -384,176 +417,225 @@
             sibling,
         )
 
+    def pair_sum(c):
+        p_push(c).wait_recv()
+        at = columns[c]
+        for b in range(ZL):
+            made[at, core, b] = (made[at, core, b].astype(F32) + from_sib[at, b].astype(F32)).astype(
+                BF16
+            )
+
+    def to_right_column(b):
+        src = made.at[right, core, b]
+        return push(src, from_left.at[b], g_send.at[b], g_recv.at[b], to_right)
+
+    def to_left_column(b):
+        src = made.at[left, core, b]
+        return push(src, from_right.at[b], h_send.at[b], h_recv.at[b], to_left)
+
+    def relay(b):
+        src = made.at[far, core, b]
+        dst = relays.at[b]
+        return push(src, dst, k_send.at[b], k_recv.at[b], to_right if b < 2 else to_left)
+
     def gather_and_apply():
-        def z_push(j):
+        def z_push(j, p):
             return push(
-                payload,
-                rows_all.at[x, zl, core],
-                z_send.at[j - 1],
-                z_recv.at[j - 1],
-                l_peer[shift[j]],
+                source(0, p),
+                slot(x, 0, p),
+                z_send.at[p, j - 1],
+                z_recv.at[p, zl],
+                {"exp": column[j] * 2 + core},
             )
 
-        def source(j):
-            return payload if j == 0 else slot(x, j)
-
-        def x_push(side, j):
-            device = (to_right, to_left)[side]
-            return push(source(j), slot(x, j), x_send.at[side, j], x_recv.at[side, j], device)
-
-        def x_arrived(side, j):
-            at = slot((left, right)[side], j)
-            push(at, at, x_send.at[side, j], x_recv.at[side, j], to_right).wait_recv()
-
-        def o_push(j):
-            at = slot(left if j < 2 else right, j)
-            return push(at, at, o_send.at[j], o_recv.at[j], to_right if j < 2 else to_left)
-
-        def o_arrived(j):
-            at = slot(far, j)
-            push(at, at, o_send.at[j], o_recv.at[j], to_right).wait_recv()
-
-        def s_push(c, j):
-            src = source(j) if c == 0 else slot(columns[c], j)
-            return push(src, slot(columns[c], j), s_send.at[c, j], s_recv.at[c, j], sibling)
-
-        def s_arrived(c, j):
-            at = rows_all.at[columns[c], column[j], 1 - core]
-            push(at, at, s_send.at[c, j], s_recv.at[c, j], sibling).wait_recv()
-
-        own = pltpu.make_async_copy(payload, rows_all.at[x, zl, core], own_sem)
+        def z_arrived(j, p):
+            at = slot(x, j, p)
+            push(at, at, z_send.at[p, j - 1], z_recv.at[p, column[j]], sibling).wait_recv()
+
+        def source(j, p):
+            return payload.at[:, pl.ds(*pieces[p])] if j == 0 else slot(x, j, p)
+
+        def x_push(way, j, p):
+            device = (to_right, to_left)[way]
+            return push(
+                source(j, p), slot(x, j, p), x_send.at[p, way, j], x_recv.at[p, way, j], device
+            )
+
+        def x_arrived(way, j, p):
+            at = slot((left, right)[way], j, p)
+            push(at, at, x_send.at[p, way, j], x_recv.at[p, way, j], to_right).wait_recv()
+
+        def o_push(j, p):
+            at = slot(left if j < 2 else right, j, p)
+            return push(at, at, o_send.at[p, j], o_recv.at[p, j], to_right if j < 2 else to_left)
+
+        def o_arrived(j, p):
+            at = slot(far, j, p)
+            push(at, at, o_send.at[p, j], o_recv.at[p, j], to_right).wait_recv()
+
+        def s_push(c):
+            at = rows_all.at[columns[c], core]
+            return push(at, at, s_send.at[c], s_recv.at[c], sibling)
+
+        def s_arrived(c):
+            at = rows_all.at[columns[c], 1 - core]
+            push(at, at, s_send.at[c], s_recv.at[c], sibling).wait_recv()
+
+        def t_push(j):
+            at = rows_all.at[far, core, column[j]]
+            return push(at, at, t_send.at[j], t_recv.at[j], sibling)
+
+        def t_arrived(j):
+            at = rows_all.at[far, 1 - core, column[j]]
+            push(at, at, t_send.at[j], t_recv.at[j], sibling).wait_recv()
+
+        def start_rows(p):
+            x_push(0, 0, p).start()
+            x_push(1, 0, p).start()
+            for j in (1, 2, 3):
+                z_push(j, p).start()
+
+        def z_forward(j, p):
+            z_arrived(j, p)
+            x_push(0, j, p).start()
+            x_push(1, j, p).start()
+
+        def x_forward(j, p):
+            for way in (0, 1):
+                x_arrived(way, j, p)
+                if (j < 2) == (way == 0):
+                    o_push(j, p).start()
+
+        square = finish_rows(0, jnp.zeros((rows, 1), F32))
+        start_rows(0)
+        finish_tail(finish_rows(1, square))
+        start_rows(1)
+        own = pltpu.make_async_copy(payload, rows_all.at[x, core, zl], own_sem)
         own.start()
-        x_push(0, 0).start()
-        x_push(1, 0).start()
-        for j in (1, 2, 3):
-            z_push(j).start()
-        s_push(0, 0).start()
-        for j in (1, 2, 3):
-            z_push(j).wait_recv()
-            x_push(0, j).start()
-            x_push(1, j).start()
-            s_push(0, j).start()
-            for side in (0, 1):
-                x_arrived(side, j - 1)
-                if (j - 1 < 2) == (side == 0):
-                    o_push(j - 1).start()
-                s_push(1 + side, j - 1).start()
+        x_forward(0, 0)
+        z_forward(1, 0)
+        x_forward(0, 1)
+        z_forward(2, 0)
+        x_forward(1, 0)
+        z_forward(3, 0)
+        x_forward(2, 0)
+        z_forward(1, 1)
+        x_forward(3, 0)
+        z_forward(2, 1)
+        x_forward(1, 1)
+        z_forward(3, 1)
         own.wait()
+        s_push(0).start()
+        x_forward(2, 1)
+        x_forward(3, 1)
+        s_push(1).start()
+        s_push(2).start()
         for copy in w_copies[1:]:
             copy.wait()
+        s_arrived(1)
+        expert(1)
+        p_push(1).start()
         for j in range(ZL):
-            s_arrived(0, j)
+            o_arrived(j, 0)
+            if j < 2:
+                o_arrived(j, 1)
+                t_push(j).start()
+        s_arrived(2)
+        expert(2)
+        p_push(2).start()
+        for j in (2, 3):
+            o_arrived(j, 1)
+            t_push(j).start()
+        pair_sum(1)
+        to_left_column(0).start()
+        to_left_column(1).start()
+        pair_sum(2)
+        to_right_column(3).start()
+        to_right_column(2).start()
+        for j in range(ZL):
+            t_arrived(j)
+        expert(3)
+        p_push(3).start()
+        s_arrived(0)
+        pair_sum(3)
+        for b in (0, 1):
+            relay(b).start()
+            relay(3 - b).start()
         expert(0)
         p_push(0).start()
-        for side in (0, 1):
-            x_arrived(side, 3)
-            if side == 1:
-                o_push(3).start()
-            s_push(1 + side, 3).start()
-        for j in range(ZL):
-            o_arrived(j)
-            s_push(3, j).start()
-        for c in (1, 2, 3):
-            for j in range(ZL):
-                s_arrived(c, j)
-            expert(c)
-            p_push(c).start()
 
         def finish():
-            for j in (1, 2, 3):
-                z_push(j).wait_send()
-            for j in range(ZL):
-                for side in (0, 1):
-                    x_push(side, j).wait_send()
-                o_push(j).wait_send()
-                for c in range(4):
-                    s_push(c, j).wait_send()
+            for p in (0, 1):
+                for j in (1, 2, 3):
+                    z_push(j, p).wait_send()
+                for j in range(ZL):
+                    for way in (0, 1):
+                        x_push(way, j, p).wait_send()
+                    o_push(j, p).wait_send()
             for c in range(4):
                 p_push(c).wait_send()
+                t_push(c).wait_send()
+                if c < 3:
+                    s_push(c).wait_send()
 
         started.append(finish)
 
     def sum_columns():
-        def pair_sum(c):
-            p_push(c).wait_recv()
-            at = columns[c]
-            for b in range(ZL):
-                made[at, core, b] = (
-                    made[at, core, b].astype(F32) + from_sib[at, b].astype(F32)
-                ).astype(BF16)
-
-        def half(ref, h):
-            return ref.at[2 * h : 2 * h + 2]
-
-        def h_push(n):
-            src, dst, device = [
-                (half(made.at[right, core], 0), half(from_left, 0), to_right),
-                (half(made.at[right, core], 1), half(from_left, 1), to_right),
-                (half(made.at[left, core], 0), half(from_right, 0), to_left),
-                (half(made.at[left, core], 1), half(from_right, 1), to_left),
-                (half(made.at[far, core], 0), relay_left, to_right),
-                (half(made.at[far, core], 1), relay_right, to_left),
-            ][n]
-            return push(src, dst, h_send.at[n], h_recv.at[n], device)
-
-        pair_sum(1)
-        h_push(2).start()
-        pair_sum(2)
-        h_push(1).start()
-        pair_sum(3)
-        h_push(4).start()
-        h_push(5).start()
+        for b in (0, 3, 1, 2):
+            relay(b).wait_recv()
+            at = right if b < 2 else left
+            made[at, core, b] = (made[at, core, b].astype(F32) + relays[b].astype(F32)).astype(BF16)
+            if b < 2:
+                to_right_column(b).start()
+            else:
+                to_left_column(b).start()
         pair_sum(0)
-        h_push(4).wait_recv()
-        for b in (0, 1):
-            made[right, core, b] = (
-                made[right, core, b].astype(F32) + relay_left[b].astype(F32)
-            ).astype(BF16)
-        h_push(0).start()
-        h_push(5).wait_recv()
-        for b in (0, 1):
-            made[left, core, 2 + b] = (
-                made[left, core, 2 + b].astype(F32) + relay_right[b].astype(F32)
-            ).astype(BF16)
-        h_push(3).start()
-        for n in (1, 2, 0, 3):
-            h_push(n).wait_recv()
-        started.append(lambda: [h_push(n).wait_send() for n in range(6)])
-
-    def sum_slices():
-        for b in range(ZL):
+
+        def to_chip(b):
+            return push(
+                ready.at[b],
+                returned.at[zl],
+                r_send.at[b],
+                r_recv.at[zl],
+                {"exp": b * 2 + core},
+            )
+
+        for b in (0, 3, 1, 2):
+            to_right_column(b).wait_recv()
+            to_left_column(b).wait_recv()
             summed = (
                 made[x, core, b].astype(F32) + from_left[b].astype(F32) + from_right[b].astype(F32)
             )
             total[b] = summed
             ready[b] = summed.astype(BF16)
 
-        def to_chip(d):
-            return push(
-                ready.at[lax.rem(zl + d, ZL)],
-                returned.at[d - 1],
-                r_send.at[d - 1],
-                r_recv.at[d - 1],
-                l_peer[d],
-            )
-
-        for d in (2, 1, 3):
-            to_chip(d).start()
-        for d in (1, 3, 2):
-            to_chip(d).wait_recv()
-        summed = total[zl]
-        for d in range(ZL - 1):
-            summed = summed + returned[d].astype(F32)
-        mix_ref[...] = summed.astype(BF16)
-        started.append(lambda: [to_chip(d).wait_send() for d in (1, 2, 3)])
+            @pl.when(zl != b)
+            def _():
+                to_chip(b).start()
+
+        mix = total[zl]
+        for j in range(1, ZL):
+            at = returned.at[column[j]]
+            push(at, at, r_send.at[j], r_recv.at[column[j]], sibling).wait_recv()
+            mix = mix + returned[column[j]].astype(F32)
+        mix_ref[...] = mix.astype(BF16)
+
+        def finish():
+            for b in range(ZL):
+                to_right_column(b).wait_send()
+                to_left_column(b).wait_send()
+                relay(b).wait_send()
+
+                @pl.when(zl != b)
+                def _():
+                    to_chip(b).wait_send()
+
+        started.append(finish)
 
     gather_and_attend()
     project()
-    sum_heads()
-    norm()
     gather_and_apply()
     sum_columns()
-    sum_slices()
     for finish in started:
         finish()
 
@@ -564,7 +646,7 @@
     rows, model = resid.shape
     hidden = wd.shape[1]
     padded = -(-model // 128) * 128
-    tiles = len(column_tiles(model, 768))
+    tiles = len(column_pieces(model, padded)[1])
     dma = pltpu.SemaphoreType.DMA
     vmem = pl.BlockSpec(memory_space=pltpu.VMEM)
     hbm = pl.BlockSpec(memory_space=pl.ANY)
@@ -587,35 +669,34 @@
             pltpu.VMEM((2, ZL, rows, model), BF16),
             pltpu.VMEM((ZL, rows, model), BF16),
             pltpu.VMEM((ZL, rows, model), BF16),
-            pltpu.VMEM((ZL - 1, rows, model), BF16),
+            pltpu.VMEM((ZL, rows, model), BF16),
             pltpu.VMEM((rows, padded), BF16),
-            pltpu.VMEM((XS, ZL, 2, rows, padded), BF16),
+            pltpu.VMEM((XS, 2, ZL, rows, padded), BF16),
             pltpu.VMEM((padded, 2 * hidden), BF16),
             pltpu.VMEM((model, hidden), BF16),
             pltpu.VMEM((XS, 2, ZL, rows, model), BF16),
             pltpu.VMEM((XS, ZL, rows, model), BF16),
             pltpu.VMEM((ZL, rows, model), BF16),
             pltpu.VMEM((ZL, rows, model), BF16),
-            pltpu.VMEM((2, rows, model), BF16),
-            pltpu.VMEM((2, rows, model), BF16),
+            pltpu.VMEM((ZL, rows, model), BF16),
             pltpu.VMEM((ZL, rows, model), F32),
             pltpu.VMEM((ZL, rows, model), BF16),
-            pltpu.VMEM((ZL - 1, rows, model), BF16),
+            pltpu.VMEM((ZL, rows, model), BF16),
             dma((4,)),
             dma,
         ]
-        + [dma((3,))] * 2
+        + [dma((ZH,))] * 2
         + [dma((4, ZH))] * 2
         + [dma((3, ZH))] * 2
         + [dma((tiles,))] * 2
+        + [dma((2, ZL))] * 2
+        + [dma((2, ZL))] * 2
+        + [dma((2, 2, ZL))] * 2
+        + [dma((2, ZL))] * 2
         + [dma((3,))] * 2
-        + [dma((3,))] * 2
-        + [dma((2, ZL))] * 2
         + [dma((ZL,))] * 2
-        + [dma((4, ZL))] * 2
         + [dma((4,))] * 2
-        + [dma((6,))] * 2
-        + [dma((3,))] * 2,
+        + [dma((ZL,))] * 8,
         compiler_params=pltpu.CompilerParams(
             collective_id=0, has_side_effects=True, vmem_limit_bytes=VMEM_BYTES
         ),

time: 112 us -> 105 us (0.938)
  Pallas kernels: 108 us -> 101 us
    pallas_call x1, Pallas kernels: 108 us -> 101 us  [layer(): pl.pallas_call(layer_kernel, out_shape=(jax.ShapeDtypeStruct((rows, model...]
where the time goes in v3:
time: 105 us; the launch traced here: 104 us
  Pallas kernels  101 us (96%)
  local copies, waits for them, and re-layouts  3.07 us (3%)
    pallas_call x1, Pallas kernels, layer(): pl.pallas_call(layer_kernel, out_shape=(jax.ShapeDtypeStruct((rows, model...  101 us
    unnamed x2, local copies, waits for them, and re-layouts  3.07 us

profile of v3, /device:TPU:58, one launch (start us, length us, event | category | flops | bytes accessed | tf_op | source)
XLA Modules:
  0.0 104.4 jit_solution(5136296911978141977)
XLA Ops:
  0.6 100.7 %shard_map.104 = (bf16[16,2880]{1,0:T(8,128)(2,1)}, bf16[16,2880]{1,0:T(8,128)(2,1)}) custom-call(bf16[128,512]{1,0:T(8,128)(2,1)} %bitcast.19, bf16[128,128]{1,0:T(8,128)(2,1)} %bitcast.23, bf16[2880,512]{1,0:T(8,128)(2,1)} %bitcast.17, bf16[16,2880]{1,0:T(8,128)(2,1)} %bitcast.20, f32[2880]{0:T(1024)} %gain_ref.1, s32[2,16]{1,0:T(2,128)} %bitcast.24, ...), custom_call_target="tpu_custom_call" | custom-call | tf_op jit(solution)/shard_map/pallas_call | solution.py:653
  101.4 1.5 %copy.13 = bf16[1,16,2880]{2,1,0:T(8,128)(2,1)} copy(bf16[1,16,2880]{2,1,0:T(8,128)(2,1)} %bitcast.22) | data formatting | bytes 184320
  102.9 1.5 %copy.14 = bf16[1,16,2880]{2,1,0:T(8,128)(2,1)} copy(bf16[1,16,2880]{2,1,0:T(8,128)(2,1)} %bitcast.21) | data formatting | bytes 184320

commit v4 on v3

--- a/solution.py
+++ b/solution.py
@@ -157,6 +157,12 @@
     shift = [0, 1, 3, 2]
     started = []
 
+    def settle():
+        for finish in started:
+            finish()
+        started.clear()
+
+
     def gather_and_attend():
         column = [lax.rem(z + ZH - s, ZH) for s in shift]
         sends_up = y < YS - 1
@@ -324,6 +330,7 @@
                 if start + size == min(sum(pieces[piece]), model):
                     for j in (1, 2, 3):
                         to_chip(j, piece).start()
+        settle()
         started.append(lambda: [to_sibling(n).wait_send() for n in range(len(tiles))])
         started.append(
             lambda: [to_chip(j, piece).wait_send() for j in (1, 2, 3) for piece in (0, 1)]
@@ -613,6 +620,11 @@
             def _():
                 to_chip(b).start()
 
+        settle()
+        for b in range(ZL):
+            to_right_column(b).wait_send()
+            to_left_column(b).wait_send()
+            relay(b).wait_send()
         mix = total[zl]
         for j in range(1, ZL):
             at = returned.at[column[j]]
@@ -622,9 +634,6 @@
 
         def finish():
             for b in range(ZL):
-                to_right_column(b).wait_send()
-                to_left_column(b).wait_send()
-                relay(b).wait_send()
 
                 @pl.when(zl != b)
                 def _():
@@ -636,8 +645,7 @@
     project()
     gather_and_apply()
     sum_columns()
-    for finish in started:
-        finish()
+    settle()
 
 
 def layer(q, kv, wo, resid, gain, ids, rw, wgu, wd):

time: 105 us -> 105 us (level)
  no operation moved by 1% of the time
where the time goes in v4:
time: 105 us; the launch traced here: 104 us
  Pallas kernels  101 us (96%)
  local copies, waits for them, and re-layouts  3.07 us (3%)
    pallas_call x1, Pallas kernels, layer(): pl.pallas_call(layer_kernel, out_shape=(jax.ShapeDtypeStruct((rows, model...  101 us
    unnamed x2, local copies, waits for them, and re-layouts  3.07 us

profile of v4, /device:TPU:58, one launch (start us, length us, event | category | flops | bytes accessed | tf_op | source)
XLA Modules:
  0.0 104.4 jit_solution(11910583947896230917)
XLA Ops:
  0.6 100.7 %shard_map.104 = (bf16[16,2880]{1,0:T(8,128)(2,1)}, bf16[16,2880]{1,0:T(8,128)(2,1)}) custom-call(bf16[128,512]{1,0:T(8,128)(2,1)} %bitcast.19, bf16[128,128]{1,0:T(8,128)(2,1)} %bitcast.23, bf16[2880,512]{1,0:T(8,128)(2,1)} %bitcast.17, bf16[16,2880]{1,0:T(8,128)(2,1)} %bitcast.20, f32[2880]{0:T(1024)} %gain_ref.1, s32[2,16]{1,0:T(2,128)} %bitcast.24, ...), custom_call_target="tpu_custom_call" | custom-call | tf_op jit(solution)/shard_map/pallas_call | solution.py:661
  101.4 1.5 %copy.13 = bf16[1,16,2880]{2,1,0:T(8,128)(2,1)} copy(bf16[1,16,2880]{2,1,0:T(8,128)(2,1)} %bitcast.22) | data formatting | bytes 184320
  102.9 1.5 %copy.14 = bf16[1,16,2880]{2,1,0:T(8,128)(2,1)} copy(bf16[1,16,2880]{2,1,0:T(8,128)(2,1)} %bitcast.21) | data formatting | bytes 184320
